TPU v7x, 768 devices: a whole 4x8x12 slice. The times are simulated.
768 devices in a mesh: row: 32 (over y, z_lo), col: 24 (over x, z_hi, core).
Axes of the slice: x: 4, y: 8, z: 12 (z_hi: 3, z_lo: 4; z = z_hi * 4 + z_lo), core: 2. Of those that a mesh axis runs over, the one named last changes fastest.
Arguments:
- curl_tiles: bfloat16 [32, 768, 24576], P(None, 'col', 'row'), may hold values from -0.00024414062 to 0.00024414062
- gradient: bfloat16 [24576, 1536], P(('row', 'col')), may hold values from -6 to 6
- a_pattern: int32 [192, 192], replicated, may hold values 0 or 1
- g_pattern: int32 [192, 12], replicated, may hold values 0 or 1
Outputs:
- galerkin: float32 [1536, 1536], P('row', 'col')
Inputs may be any that keep to these rules, and one draw needn't show every extreme that they name: `a_pattern`: 1 keeps a block in the pattern, 0 leaves it out. `g_pattern`: 1 keeps a block in the pattern, 0 leaves it out.
All inputs are finite; a program needn't handle non-finite values.
Results may differ from a plain program's by a relative error of at most 0.0003.
Values may be sent and summed in bfloat16 or wider, within the bound.
A program may use at most 32 MiB of HBM per device.

v0:
```python
import jax
import jax.numpy as jnp
from jax import lax
from jax.sharding import PartitionSpec as P

BLOCK = 128


def block_hits(position, block_total):
    return (position[:, None] // BLOCK == jnp.arange(block_total, dtype=jnp.int32)[None, :]).astype(
        jnp.float32
    )


def body(curl_tiles, gradient, a_pattern, g_pattern):
    row_count = lax.axis_size("row")
    row_pos = lax.axis_index("row")
    col_pos = lax.axis_index("col")
    rows_here = curl_tiles.shape[1]
    span_rows = curl_tiles.shape[2]
    fine_blocks = a_pattern.shape[0]
    strided_total = row_count * rows_here
    offsets = jnp.arange(rows_here, dtype=jnp.int32)
    column_index = (
        jnp.arange(row_count, dtype=jnp.int32)[:, None] * span_rows
        + col_pos * rows_here
        + offsets[None, :]
    ).reshape(-1)
    row_index = row_pos * span_rows + jnp.arange(span_rows, dtype=jnp.int32)
    own_index = row_pos * span_rows + col_pos * rows_here + offsets
    picked = jnp.dot(block_hits(row_index, fine_blocks), a_pattern.astype(jnp.float32))
    keep_a = jnp.dot(block_hits(column_index, fine_blocks), picked.T)
    masked_a = curl_tiles.reshape(strided_total, span_rows) * keep_a.astype(jnp.bfloat16)
    keep_g = jnp.dot(block_hits(own_index, fine_blocks), g_pattern.astype(jnp.float32))
    masked_g = gradient * jnp.repeat(keep_g, BLOCK, axis=1).astype(jnp.bfloat16)
    g_group = lax.all_gather(masked_g, "col", axis=0, tiled=True)
    g_strided = lax.all_gather(masked_g, "row", axis=0, tiled=True)
    portion = g_strided
    product_t = lax.psum_scatter(
        lax.dot_general(
            portion, masked_a, (((0,), (0,)), ((), ())), preferred_element_type=jnp.float32
        ),
        "col",
        scatter_dimension=0,
        tiled=True,
    )
    portion = g_group.astype(jnp.float32)
    return lax.psum_scatter(
        lax.dot_general(
            portion,
            product_t,
            (((0,), (1,)), ((), ())),
            precision=lax.Precision.HIGHEST,
            preferred_element_type=jnp.float32,
        ),
        "row",
        scatter_dimension=0,
        tiled=True,
    )


def solution(mesh):
    placed = (P(None, "col", "row"), P(("row", "col"), None), P(), P())
    return jax.shard_map(
        body, mesh=mesh, in_specs=placed, out_specs=P("row", "col"), check_vma=False
    )
```

profile of v0, /device:TPU:4, one launch (start us, length us, event | category | flops | bytes accessed | tf_op | source)
XLA Modules:
  0.0 598.0 jit_solution(528074421568182991)
XLA Ops:
  6.5 0.0 all-gather.5.cloned.1.call-start
  6.5 0.9 convolution_convert_fusion.1
  7.5 0.1 copy.6
  7.6 0.1 broadcast_in_dim.2
  7.7 1.6 bitcast_multiply_fusion.1
  9.3 0.0 all-gather.5.cloned.1.call-update
  9.3 0.0 all-gather.3.cloned.1.call-start
  9.3 0.7 all-gather.3.cloned.1.call-update
  10.0 0.0 reduce-scatter.3.cloned.1.call-start
  10.1 0.1 iota_add_fusion
  10.2 0.1 add.97
  10.3 2.4 bitcast_multiply_fusion
  12.7 169.3 %all-gather.5.cloned.1.call-done = bf16[1024,1536]{1,0:T(8,128)(2,1)} async-done(((bf16[32,1536]{1,0:T(8,128)(2,1)}), bf16[1024,1536]{1,0:T(8,128)(2,1)}) %all-gather.5.cloned.1.call-update) | async-done | bytes 3145744 | tf_op jit(solution)/shard_map/all_gather | solution.py:37
  182.0 6.7 %fusion.14 = f32[1536,768]{1,0:T(8,128)} fusion(bf16[1024,1536]{1,0:T(8,128)(2,1)} %all-gather.5.cloned.1.call-done, bf16[1024,768]{1,0:T(8,128)(2,1)S(1)} %bitcast_multiply_fusion), kind=kOutput, calls=%fused_computation.35 | convolution fusion | flops 2415919104 | bytes 9437184 | tf_op jit(solution)/shard_map/dot_general | solution.py:40
  188.7 0.0 reduce-scatter.3.cloned.1.call-update
  188.7 0.0 reduce-scatter.5.cloned.1.call-start
  188.8 76.1 %all-gather.3.cloned.1.call-done = bf16[768,1536]{1,0:T(8,128)(2,1)} async-done(((bf16[32,1536]{1,0:T(8,128)(2,1)}), bf16[768,1536]{1,0:T(8,128)(2,1)}) %all-gather.3.cloned.1.call-update) | async-done | bytes 2359312 | tf_op jit(solution)/shard_map/all_gather | solution.py:36
  264.9 158.4 %reduce-scatter.3.cloned.1.call-done = f32[64,768]{1,0:T(8,128)} async-done(((f32[1536,768]{1,0:T(8,128)}), f32[64,768]{1,0:T(8,128)}) %reduce-scatter.3.cloned.1.call-update) | async-done | bytes 196624 | tf_op jit(solution)/shard_map/reduce_scatter | solution.py:39
  423.3 5.1 fusion.15
  428.4 0.0 reduce-scatter.5.cloned.1.call-update
  428.4 163.1 %reduce-scatter.5.cloned.1.call-done = f32[48,64]{1,0:T(8,128)} async-done(((f32[1536,64]{1,0:T(8,128)}), f32[48,64]{1,0:T(8,128)}) %reduce-scatter.5.cloned.1.call-update) | async-done | bytes 12304 | tf_op jit(solution)/shard_map/reduce_scatter | solution.py:48
  (4 shorter events, 0.0 us)
Async XLA Ops:
  6.5 175.5 %all-gather.5.cloned.1.call-start = ((), (), s32[]{:S(2)}) async-start(), calls=%async_computation.3 | async-start | bytes 3244032 | tf_op jit(solution)/shard_map/all_gather | solution.py:37
  9.3 255.6 %all-gather.3.cloned.1.call-start = ((), (), s32[]{:S(2)}) async-start(), calls=%async_computation.2 | async-start | bytes 2457600 | tf_op jit(solution)/shard_map/all_gather | solution.py:36
  10.0 413.2 %reduce-scatter.3.cloned.1.call-start = ((), (), s32[]{:S(2)}) async-start(), calls=%async_computation.4 | async-start | bytes 4915200 | tf_op jit(solution)/shard_map/reduce_scatter | solution.py:39
  188.7 402.8 %reduce-scatter.5.cloned.1.call-start = ((), (), s32[]{:S(2)}) async-start(), calls=%async_computation.5 | async-start | bytes 811008 | tf_op jit(solution)/shard_map/reduce_scatter | solution.py:48
Sparse Core Ops, SparseCore 0:
  9.7 172.2 all-gather.4
  186.1 78.8 all-gather.2
  270.7 152.5 reduce-scatter.2
  428.6 162.9 reduce-scatter.4
where the time goes:
time: 598 us
  waiting for transfers between devices  568 us (95%)
  matrix products  15.1 us (3%)
  between operations  13.2 us (2%)
    all_gather x1, waiting for transfers between devices, body(): g_strided = lax.all_gather(masked_g, 'row', axis=0, tiled=True)  169 us
    reduce_scatter x1, waiting for transfers between devices, body(): lax.psum_scatter(lax.dot_general(portion, product_t, (((0,), (1,)), ((),...  163 us
    reduce_scatter x1, waiting for transfers between devices, body(): lax.psum_scatter(lax.dot_general(portion, masked_a, (((0,), (0,)), ((), (...  158 us
    all_gather x1, waiting for transfers between devices, body(): g_group = lax.all_gather(masked_g, 'col', axis=0, tiled=True)  76.1 us
  transfers between devices with their start and end apart: 4, of which 4 were waited for; matrix products, arithmetic and copies ran while one was open for 2% of the time, Pallas kernels for 0%

commit v1 on v0

v1 whole, which is shorter than its diff:
```python
import jax
import jax.numpy as jnp
from jax import lax
from jax.experimental import pallas as pl
from jax.experimental.pallas import tpu as pltpu
from jax.sharding import PartitionSpec as P

BLOCK = 128
NX, NY, NZL, NZH, NC = 4, 8, 4, 3, 2
NT = 3
F32, BF16 = jnp.float32, jnp.bfloat16

SITES = {}
TOTAL = 0


def site(name, count=1):
    global TOTAL
    SITES[name] = TOTAL
    TOTAL += count


for t in range(NT):
    site(("z", t), 4)
    for hop in range(1, 5):
        for side in "RL":
            site(("y", t, hop, side), 2)
    site(("cx", t))
    for side in "RL":
        site(("x", t, side), 3)
        site(("q", t, side), 4)
    site(("qc", t))
    site(("f", t), 4)
site("gz", 3)
for side in "RL":
    site(("gx", side), 2)
site("out")


def kernel(a_hbm, g_ref, ap_ref, gp_ref, out_ref, a_buf, at, gm, gs, gr, grt, po, pm, cx, xr, q, qcr, yr, zr, fin, fx,
           a_sem, ssem, rsem):
    row, col = lax.axis_index("row"), lax.axis_index("col")
    y, zl = row // NZL, row % NZL
    x, zh, core = col // (NZH * NC), (col // NC) % NZH, col % NC
    sib = 1 - core

    def mod(v, n):
        return lax.rem(v + n, n)

    def dev(dx=0, dy=0, dzl=0, dzh=0, other=False):
        yy, zz = mod(y + dy, NY), mod(zl + dzl, NZL)
        xx, hh = mod(x + dx, NX), mod(zh + dzh, NZH)
        cc = sib if other else core
        return (yy * NZL + zz, xx * (NZH * NC) + hh * NC + cc)

    drains = []

    def send(name, k, src, dst, to):
        i = SITES[name] + k
        copy = pltpu.make_async_remote_copy(
            src_ref=src, dst_ref=dst, send_sem=ssem.at[i], recv_sem=rsem.at[i],
            device_id=to, device_id_type=pl.DeviceIdType.MESH)
        copy.start()
        drains.append(copy)

    def arrived(name, k, dst):
        i = SITES[name] + k
        pltpu.make_async_remote_copy(
            src_ref=dst, dst_ref=dst, send_sem=ssem.at[i], recv_sem=rsem.at[i],
            device_id=dev(dy=1), device_id_type=pl.DeviceIdType.MESH).wait_recv()

    def drain(keep=0):
        while len(drains) > keep:
            drains.pop(0).wait_send()

    load_a = pltpu.make_async_copy(a_hbm, a_buf, a_sem)
    load_a.start()

    barrier = pltpu.get_barrier_semaphore()
    peers = [dev(dzl=i, dzh=h) for h in range(NZH) for i in range(NZL) if i or h]
    peers += [dev(dy=1), dev(dy=-1), dev(dx=1), dev(dx=-1), dev(other=True)]
    for peer in peers:
        pl.semaphore_signal(barrier, inc=1, device_id=peer, device_id_type=pl.DeviceIdType.MESH)

    own_block = row * 6 + col // 4
    keep = gp_ref[pl.ds(own_block, 1), :].astype(F32)
    for p in range(12):
        part = slice(p * BLOCK, (p + 1) * BLOCK)
        gm[:, part] = (g_ref[:, part].astype(F32) * jnp.broadcast_to(keep[:, p:p + 1], (32, BLOCK))).astype(BF16)
    me_m = x * NZH + zh
    gr[pl.ds(pl.multiple_of(me_m * 32, 32), 32), :] = gm[...]
    for t in range(NT):
        jj = mod(zh + 1 + t, NZH)
        for xx in range(NX):
            off = pl.multiple_of(xx * 384 + jj * BLOCK, BLOCK)
            gs[t, y, zl, :, xx * BLOCK:(xx + 1) * BLOCK] = gm[:, pl.ds(off, BLOCK)]

    pl.semaphore_wait(barrier, len(peers))

    def send_z(t):
        for i in range(1, NZL):
            send(("z", t), i, gs.at[t, y, zl], gs.at[t, y, zl], dev(dzl=i))

    def y_part(t, yy, p):
        return gs.at[t, mod(yy + NY, NY), pl.ds(2 * p, 2)]

    def a1(t):
        for i in range(1, NZL):
            arrived(("z", t), i, gs.at[t, y, mod(zl - i, NZL)])
        for p in range(2):
            ref = y_part(t, y, p)
            send(("y", t, 1, "R"), p, ref, ref, dev(dy=1))
            send(("y", t, 1, "L"), p, ref, ref, dev(dy=-1))

    def forward(t, hop):
        for p in range(2):
            ref = y_part(t, y - (hop - 1), p)
            arrived(("y", t, hop - 1, "R"), p, ref)
            if hop < 4 or p == 0:
                send(("y", t, hop, "R"), p, ref, ref, dev(dy=1))
            ref = y_part(t, y + (hop - 1), p)
            arrived(("y", t, hop - 1, "L"), p, ref)
            if hop < 4 or p == 1:
                send(("y", t, hop, "L"), p, ref, ref, dev(dy=-1))

    def a5(t):
        arrived(("y", t, 4, "R"), 0, y_part(t, y - 4, 0))
        arrived(("y", t, 4, "L"), 1, y_part(t, y + 4, 1))

    def prepare_a():
        load_a.wait()
        ap = ap_ref[...].astype(F32).astype(BF16)
        want = lax.broadcasted_iota(jnp.int32, (8, 192), 0) + row * 6
        pick = jnp.where(want == lax.broadcasted_iota(jnp.int32, (8, 192), 1), 1.0, 0.0).astype(BF16)
        rows = jnp.dot(pick, ap, preferred_element_type=F32).astype(BF16)
        want = (lax.broadcasted_iota(jnp.int32, (192, 1024), 1) // 32) * 6 + col // 4
        pick = jnp.where(want == lax.broadcasted_iota(jnp.int32, (192, 1024), 0), 1.0, 0.0).astype(BF16)
        mask = jnp.dot(rows, pick, preferred_element_type=F32)
        for b in range(6):
            block = a_buf[:, :, b * BLOCK:(b + 1) * BLOCK].reshape(1024, BLOCK)
            turned = (block.T.astype(F32) * mask[b:b + 1, :]).astype(BF16)
            for i in range(4):
                at[i % 2, (2 * b + i // 2) * 32:(2 * b + i // 2 + 1) * 32, :] = turned[i * 32:(i + 1) * 32]

    def g0():
        own = gr.at[pl.ds(pl.multiple_of(me_m * 32, 32), 32)]
        for h in range(1, NZH):
            send("gz", h, own, own, dev(dzh=h))

    def gx_rows(xx, first=0, count=96):
        return gr.at[pl.ds(pl.multiple_of(mod(xx + NX, NX) * 96 + first, 16), count)]

    def g1():
        for h in range(1, NZH):
            m = x * NZH + mod(zh - h, NZH)
            arrived("gz", h, gr.at[pl.ds(pl.multiple_of(m * 32, 32), 32)])
        send(("gx", "R"), 0, gx_rows(x), gx_rows(x), dev(dx=1))
        send(("gx", "L"), 0, gx_rows(x), gx_rows(x), dev(dx=-1))

    def g2():
        arrived(("gx", "R"), 0, gx_rows(x - 1))
        send(("gx", "R"), 1, gx_rows(x - 1, 0, 48), gx_rows(x - 1, 0, 48), dev(dx=1))
        arrived(("gx", "L"), 0, gx_rows(x + 1))
        send(("gx", "L"), 1, gx_rows(x + 1, 48, 48), gx_rows(x + 1, 48, 48), dev(dx=-1))

    def g3():
        arrived(("gx", "R"), 1, gx_rows(x - 2, 0, 48))
        arrived(("gx", "L"), 1, gx_rows(x + 2, 48, 48))
        for b in range(3):
            part = slice(b * BLOCK, (b + 1) * BLOCK)
            grt[:, part] = gr[part, :].T

    def product(t, half, out):
        for n in range(2):
            b = gs[t, :, :, :, n * 256:(n + 1) * 256].reshape(1024, 256)
            r = jnp.dot(at[half], b, preferred_element_type=F32)
            out[t, 2 * n] = r[:, :BLOCK]
            out[t, 2 * n + 1] = r[:, BLOCK:]

    def r0(t):
        product(t, sib, po)
        send(("cx", t), 0, po.at[t], cx.at[t], dev(other=True))
        product(t, core, pm)

    xp, xm, xo = mod(x + 1, NX), mod(x - 1, NX), mod(x + 2, NX)
    A, B = pl.ds(0, 192), pl.ds(192, 192)

    def r1(t):
        arrived(("cx", t), 0, cx.at[t])
        pm[t, xo] += cx[t, xo]
        send(("x", t, "R"), 0, pm.at[t, xo, A], xr.at[t, 0], dev(dx=1))
        send(("x", t, "L"), 0, pm.at[t, xo, B], xr.at[t, 3], dev(dx=-1))
        pm[t, xp] += cx[t, xp]
        send(("x", t, "R"), 1, pm.at[t, xp, B], xr.at[t, 1], dev(dx=1))
        pm[t, xm] += cx[t, xm]
        send(("x", t, "L"), 1, pm.at[t, xm, A], xr.at[t, 4], dev(dx=-1))
        pm[t, x] += cx[t, x]

    def r2(t):
        arrived(("x", t, "R"), 0, xr.at[t, 0])
        pm[t, xp, A] += xr[t, 0]
        send(("x", t, "R"), 2, pm.at[t, xp, A], xr.at[t, 2], dev(dx=1))
        arrived(("x", t, "L"), 0, xr.at[t, 3])
        pm[t, xm, B] += xr[t, 3]
        send(("x", t, "L"), 2, pm.at[t, xm, B], xr.at[t, 5], dev(dx=-1))

    def r3(t):
        for k in (1, 2):
            arrived(("x", t, "R"), k, xr.at[t, k])
            arrived(("x", t, "L"), k, xr.at[t, 3 + k])
        total = pm[t, x]
        upper = total[:192] + (xr[t, 2] + xr[t, 4])
        lower = total[192:] + (xr[t, 1] + xr[t, 5])
        total = jnp.concatenate([upper, lower], axis=0)
        high = total.astype(BF16)
        low = (total - high.astype(F32)).astype(BF16)
        r = jnp.dot(grt[...], jnp.concatenate([high, low], axis=1), preferred_element_type=F32)
        r = (r[:, :BLOCK] + r[:, BLOCK:]).reshape(32, 2, 24, BLOCK)
        q[t, 0] = r[:, 0]
        q[t, 1] = r[:, 1]
        send(("qc", t), 0, q.at[t, sib], qcr.at[t], dev(other=True))

    def q_rows(t, dy):
        return q.at[t, core, pl.ds(mod(y + dy + NY, NY) * NZL, NZL)]

    def q_half(t, dy, p):
        return q.at[t, core, pl.ds(mod(y + dy + NY, NY) * NZL + 2 * p, 2)]

    def r4(t):
        arrived(("qc", t), 0, qcr.at[t])
        q[t, core] += qcr[t]
        send(("q", t, "R"), 0, q_half(t, 4, 0), yr.at[t, 0, 0, pl.ds(0, 2)], dev(dy=1))
        send(("q", t, "L"), 0, q_half(t, -4, 1), yr.at[t, 1, 0, pl.ds(2, 2)], dev(dy=-1))

    def y_step(t, k):
        if k == 1:
            arrived(("q", t, "R"), 0, yr.at[t, 0, 0, pl.ds(0, 2)])
            q_half(t, 3, 0)[...] += yr[t, 0, 0, 0:2]
        else:
            arrived(("q", t, "R"), k - 1, yr.at[t, 0, k - 1])
            q_rows(t, 4 - k)[...] += yr[t, 0, k - 1]
        send(("q", t, "R"), k, q_rows(t, 4 - k), yr.at[t, 0, k], dev(dy=1))
        if k == 1:
            arrived(("q", t, "L"), 0, yr.at[t, 1, 0, pl.ds(2, 2)])
            q_half(t, -3, 1)[...] += yr[t, 1, 0, 2:4]
        else:
            arrived(("q", t, "L"), k - 1, yr.at[t, 1, k - 1])
            q_rows(t, k - 4)[...] += yr[t, 1, k - 1]
        send(("q", t, "L"), k, q_rows(t, k - 4), yr.at[t, 1, k], dev(dy=-1))

    def r8(t):
        arrived(("q", t, "R"), 3, yr.at[t, 0, 3])
        arrived(("q", t, "L"), 3, yr.at[t, 1, 3])
        fin[t] = q_rows(t, 0)[...] + (yr[t, 0, 3] + yr[t, 1, 3])
        for i in range(NZL):
            if t < 2 or i:
                send(("f", t), i, fin.at[t, mod(zl + i, NZL)], zr.at[t, i], dev(dzl=i, dzh=t + 1))

    def finish():
        total = fin[2, zl]
        for t in range(NT):
            for i in range(NZL):
                if t < 2 or i:
                    arrived(("f", t), i, zr.at[t, i])
                    total = total + zr[t, i]
        fx[0] = total
        send("out", 0, fx.at[0], fx.at[1], dev(other=True))
        arrived("out", 0, fx.at[1])
        theirs = fx[1]
        mine = jnp.where(core == 0, total[:, :64], total[:, 64:])
        theirs = jnp.where(core == 0, theirs[:, :64], theirs[:, 64:])
        out_ref[0:24, :] = jnp.where(core == 0, mine, theirs)
        out_ref[24:48, :] = jnp.where(core == 0, theirs, mine)

    for t in range(NT):
        send_z(t)
    g0()
    a1(0)
    prepare_a()
    forward(0, 2)
    g1()
    forward(0, 3)
    forward(0, 4)
    a1(1)
    g2()
    a5(0)
    r0(0)
    forward(1, 2)
    r1(0)
    forward(1, 3)
    r2(0)
    forward(1, 4)
    a1(2)
    g3()
    r3(0)
    a5(1)
    r0(1)
    r4(0)
    forward(2, 2)
    r1(1)
    y_step(0, 1)
    forward(2, 3)
    r2(1)
    y_step(0, 2)
    forward(2, 4)
    r3(1)
    y_step(0, 3)
    a5(2)
    r0(2)
    r8(0)
    r4(1)
    r1(2)
    y_step(1, 1)
    r2(2)
    y_step(1, 2)
    r3(2)
    y_step(1, 3)
    r4(2)
    r8(1)
    for k in (1, 2, 3):
        y_step(2, k)
    r8(2)
    finish()
    drain()


def body(curl_tiles, gradient, a_pattern, g_pattern):
    vmem = pl.BlockSpec(memory_space=pltpu.VMEM)
    return pl.pallas_call(
        kernel,
        out_shape=jax.ShapeDtypeStruct((48, 64), F32),
        in_specs=[pl.BlockSpec(memory_space=pl.ANY), vmem, vmem, vmem],
        out_specs=vmem,
        scratch_shapes=[
            pltpu.VMEM((32, 32, 768), BF16),
            pltpu.VMEM((2, 384, 1024), BF16),
            pltpu.VMEM((32, 1536), BF16),
            pltpu.VMEM((NT, NY, NZL, 32, 512), BF16),
            pltpu.VMEM((384, 1536), BF16),
            pltpu.VMEM((1536, 384), BF16),
            pltpu.VMEM((NT, NX, 384, BLOCK), F32),
            pltpu.VMEM((NT, NX, 384, BLOCK), F32),
            pltpu.VMEM((NT, NX, 384, BLOCK), F32),
            pltpu.VMEM((NT, 6, 192, BLOCK), F32),
            pltpu.VMEM((NT, 2, 32, 24, BLOCK), F32),
            pltpu.VMEM((NT, 32, 24, BLOCK), F32),
            pltpu.VMEM((NT, 2, 4, NZL, 24, BLOCK), F32),
            pltpu.VMEM((NT, NZL, 24, BLOCK), F32),
            pltpu.VMEM((NT, NZL, 24, BLOCK), F32),
            pltpu.VMEM((2, 24, BLOCK), F32),
            pltpu.SemaphoreType.DMA,
            pltpu.SemaphoreType.DMA((TOTAL,)),
            pltpu.SemaphoreType.DMA((TOTAL,)),
        ],
        compiler_params=pltpu.CompilerParams(
            collective_id=0, has_side_effects=True, vmem_limit_bytes=48 * 1024 * 1024),
    )(curl_tiles, gradient, a_pattern, g_pattern)


def solution(mesh):
    placed = (P(None, "col", "row"), P(("row", "col"), None), P(), P())
    return jax.shard_map(
        body, mesh=mesh, in_specs=placed, out_specs=P("row", "col"), check_vma=False
    )
```

time: 598 us -> 116 us (0.19)
  the two profiles are of different devices: /device:TPU:4 before, /device:TPU:1 now
where the time goes in v1:
time: 116 us; the launch traced here: 115 us
  Pallas kernels  111 us (96%)
  local copies, waits for them, and re-layouts  4.65 us (4%)
    pallas_call x1, Pallas kernels, body(): pl.pallas_call(kernel, out_shape=jax.ShapeDtypeStruct((48, 64), F32), in_...  111 us
    unnamed x8, local copies, waits for them, and re-layouts  4.65 us

profile of v1, /device:TPU:1, one launch (start us, length us, event | category | flops | bytes accessed | tf_op | source)
XLA Modules:
  0.0 115.3 jit_solution(7984547740400132257)
XLA Ops:
  0.0 0.8 copy.5.gp_ref
  0.8 0.0 copy-start
  0.8 1.4 %copy-done = bf16[32,32,768]{2,1,0:T(8,128)(2,1)S(1)} copy-done((bf16[32,32,768]{2,1,0:T(8,128)(2,1)S(1)}, bf16[32,32,768]{2,1,0:T(8,128)(2,1)}, u32[]{:S(2)}) %copy-start) | copy-done | bytes 1572888
  2.2 0.0 copy-start.1
  2.2 0.9 copy-done.1
  3.2 0.0 copy-start.2
  3.2 0.9 copy-done.2
  4.1 110.7 %shard_map.46 = f32[48,64]{1,0:T(8,128)S(1)} custom-call(bf16[32,32,768]{2,1,0:T(8,128)(2,1)S(1)} %copy-done, bf16[32,1536]{1,0:T(8,128)(2,1)S(1)} %copy-done.2, s32[192,192]{1,0:T(8,128)S(1)} %copy-done.1, s32[192,12]{1,0:T(8,128)S(1)} %copy.5.gp_ref), custom_call_target="tpu_custom_call" | custom-call | tf_op jit(solution)/shard_map/pallas_call | solution.py:329
  114.7 0.6 copy.7
Async XLA Ops:
  0.8 1.4 %copy-start = (bf16[32,32,768]{2,1,0:T(8,128)(2,1)S(1)}, bf16[32,32,768]{2,1,0:T(8,128)(2,1)}, u32[]{:S(2)}) copy-start(bf16[32,32,768]{2,1,0:T(8,128)(2,1)} %a_hbm.1) | copy-start | bytes 4718596
  2.2 0.9 copy-start.1
  3.2 0.9 copy-start.2

commit v2 on v0

v2 whole, which is shorter than its diff:
```python
import jax
import jax.numpy as jnp
from jax import lax
from jax.experimental import pallas as pl
from jax.experimental.pallas import tpu as pltpu
from jax.sharding import PartitionSpec as P

BLOCK = 128
NX, NY, NZL, NZH, NC = 4, 8, 4, 3, 2
NT = 3
F32, BF16 = jnp.float32, jnp.bfloat16
MESH = pl.DeviceIdType.MESH

GATHER = [(0, 0, 256), (0, 256, 256), (1, 0, 256), (1, 256, 256), (2, 0, 256), (2, 256, 256)]
REDUCE = [(0, 0, 1, False, False), (0, 1, 1, False, False), (1, 0, 1, False, False), (1, 1, 1, False, False), (2, 0, 1, True, True), (2, 1, 1, True, True)]

SITES = {}
TOTAL = 0


def site(name, count=1):
    global TOTAL
    SITES[name] = TOTAL
    TOTAL += count


for a in range(len(GATHER)):
    site(("z", a), 4)
    for hop in range(1, 5):
        for side in "RL":
            site(("y", a, hop, side), 2)
for u in range(len(REDUCE)):
    site(("cx", u))
    site(("x", u), 6)
    site(("qc", u))
    site(("q", u), 8)
site("f", 12)
site("gz", 3)
for side in "RL":
    site(("gx", side), 2)


def kernel(a_hbm, g_hbm, ap_hbm, gp_hbm, out_ref, a_buf, g_buf, ap_buf, gp_buf, at, gm, gs, gr, grt, po, pm, cx, xr,
           q, qcr, yr, zr, fin, load_sem, ssem, rsem):
    row, col = lax.axis_index("row"), lax.axis_index("col")
    y, zl = row // NZL, row % NZL
    x, zh, core = col // (NZH * NC), (col // NC) % NZH, col % NC
    sib = 1 - core

    places = {"x": (x, NX), "y": (y, NY), "zl": (zl, NZL), "zh": (zh, NZH)}
    known = {}

    def near(axis, d):
        here, n = places[axis]
        if d % n == 0:
            return here
        if (axis, d % n) not in known:
            known[axis, d % n] = lax.rem(here + d % n, n)
        return known[axis, d % n]

    def at_device(xx, yy, zz, hh, cc):
        return (yy * NZL + zz, xx * (NZH * NC) + hh * NC + cc)

    def dev(dx=0, dy=0, dzl=0, dzh=0, other=False):
        key = (dx % NX, dy % NY, dzl % NZL, dzh % NZH, other)
        if key not in known:
            known[key] = at_device(near("x", dx), near("y", dy), near("zl", dzl), near("zh", dzh), sib if other else core)
        return known[key]

    loads = [pltpu.make_async_copy(src, dst, load_sem.at[i]) for i, (src, dst) in enumerate(
        [(g_hbm, g_buf), (gp_hbm, gp_buf), (ap_hbm, ap_buf), (a_hbm, a_buf)])]
    for load in loads:
        load.start()

    barrier = pltpu.get_barrier_semaphore()
    peers = [dev(dzh=h) for h in range(1, NZH)] + [dev(dzl=i, other=o) for i in range(NZL) for o in (False, True) if i or o]
    peers += [dev(dy=1), dev(dy=-1)] + [dev(dx=d) for d in range(1, NX)]
    for peer in peers:
        pl.semaphore_signal(barrier, inc=1, device_id=peer, device_id_type=MESH)

    drains = []

    def copy_of(name, k, src, dst, to, rk=None):
        i = SITES[name] + k
        return pltpu.make_async_remote_copy(
            src_ref=src, dst_ref=dst, send_sem=ssem.at[i], recv_sem=rsem.at[i if rk is None else SITES[name] + rk],
            device_id=to, device_id_type=MESH)

    def send(name, k, src, dst, to, rk=None):
        copy = copy_of(name, k, src, dst, to, rk)
        copy.start()
        drains.append(copy)

    def arrived(name, k, dst):
        copy_of(name, k, dst, dst, dev(dy=1)).wait_recv()

    def drain():
        while drains:
            drains.pop(0).wait_send()

    loads[0].wait()
    loads[1].wait()
    own_block = row * 6 + col // 4
    lanes = lax.broadcasted_iota(jnp.int32, (12, 192), 1)
    keep = jnp.sum(jnp.where(lanes == own_block, gp_buf[...].astype(F32), 0.0), axis=1, keepdims=True)
    for p in range(12):
        part = slice(p * BLOCK, (p + 1) * BLOCK)
        gm[:, part] = (g_buf[:, part].astype(F32) * jnp.broadcast_to(keep[p:p + 1, :], (32, BLOCK))).astype(BF16)
    me_m = x * NZH + zh
    gr[pl.ds(pl.multiple_of(me_m * 32, 32), 32), :] = gm[...]
    for t in range(NT):
        jj = near("zh", 1 + t)
        blocks = [gm[:, pl.ds(pl.multiple_of(xx * 384 + jj * BLOCK, BLOCK), BLOCK)] for xx in range(NX)]
        gs[t, y, zl] = jnp.concatenate([b[:, h * 64:(h + 1) * 64] for h in range(2) for b in blocks], axis=1)

    pl.semaphore_wait(barrier, len(peers))

    def z_slab(a, zz):
        t, lane, width = GATHER[a]
        return gs.at[t, y, zz, :, pl.ds(lane, width)]

    own_pair = pl.multiple_of(zl // 2 * 2, 2)
    far_pair = pl.multiple_of(2 - own_pair, 2)
    near_step = 3 - 2 * (zl % 2)

    def pair(a, yy, p):
        t, lane, width = GATHER[a]
        return gs.at[t, near("y", yy), pl.ds(far_pair if p else own_pair, 2), :, pl.ds(lane, width)]

    def z0(a):
        for i in (1, 3, 2):
            send(("z", a), i, z_slab(a, zl), z_slab(a, zl), dev(dzl=i))

    def out_y(a, hop, p, right=True, left=True):
        if right and (hop < 4 or p == 0):
            ref = pair(a, 1 - hop, p)
            send(("y", a, hop, "R"), p, ref, ref, dev(dy=1))
        if left and (hop < 4 or p == 1):
            ref = pair(a, hop - 1, p)
            send(("y", a, hop, "L"), p, ref, ref, dev(dy=-1))

    def o1(a, p):
        if p == 0:
            arrived(("z", a), near_step, z_slab(a, zl + 1 - 2 * (zl % 2)))
        else:
            arrived(("z", a), 2, z_slab(a, near("zl", 2)))
            arrived(("z", a), 4 - near_step, z_slab(a, 3 - zl))
        out_y(a, 1, p)

    def fw(a, hop, side, p):
        arrived(("y", a, hop - 1, side), p, pair(a, 1 - hop if side == "R" else hop - 1, p))
        out_y(a, hop, p, right=side == "R", left=side == "L")

    def h5(a):
        arrived(("y", a, 3, "L"), 0, pair(a, 3, 0))
        arrived(("y", a, 3, "R"), 1, pair(a, -3, 1))
        arrived(("y", a, 4, "R"), 0, pair(a, -4, 0))
        arrived(("y", a, 4, "L"), 1, pair(a, 4, 1))

    def prepare_a():
        loads[2].wait()
        loads[3].wait()
        ap = ap_buf[...].astype(F32).astype(BF16)
        want = lax.broadcasted_iota(jnp.int32, (8, 192), 0) + row * 6
        pick = jnp.where(want == lax.broadcasted_iota(jnp.int32, (8, 192), 1), 1.0, 0.0).astype(BF16)
        rows = jnp.dot(pick, ap, preferred_element_type=F32).astype(BF16)
        want = (lax.broadcasted_iota(jnp.int32, (192, 1024), 1) // 32) * 6 + col // 4
        pick = jnp.where(want == lax.broadcasted_iota(jnp.int32, (192, 1024), 0), 1.0, 0.0).astype(BF16)
        mask = jnp.dot(rows, pick, preferred_element_type=F32)
        for b in range(6):
            block = a_buf[:, :, b * BLOCK:(b + 1) * BLOCK].reshape(1024, BLOCK)
            turned = (block.T.astype(F32) * mask[b:b + 1, :]).astype(BF16)
            for i in range(4):
                at[i % 2, (2 * b + i // 2) * 32:(2 * b + i // 2 + 1) * 32, :] = turned[i * 32:(i + 1) * 32]

    def g0():
        own = gr.at[pl.ds(pl.multiple_of(me_m * 32, 32), 32)]
        for h in range(1, NZH):
            send("gz", h, own, own, dev(dzh=h))

    def gx_rows(dx, first=0, count=96):
        return gr.at[pl.ds(pl.multiple_of(near("x", dx) * 96 + first, 16), count)]

    def g1():
        for h in range(1, NZH):
            m = x * NZH + near("zh", -h)
            arrived("gz", h, gr.at[pl.ds(pl.multiple_of(m * 32, 32), 32)])
        send(("gx", "R"), 0, gx_rows(0), gx_rows(0), dev(dx=1))
        send(("gx", "L"), 0, gx_rows(0), gx_rows(0), dev(dx=-1))

    def g2():
        arrived(("gx", "R"), 0, gx_rows(-1))
        send(("gx", "R"), 1, gx_rows(-1, 0, 48), gx_rows(-1, 0, 48), dev(dx=1))
        arrived(("gx", "L"), 0, gx_rows(1))
        send(("gx", "L"), 1, gx_rows(1, 48, 48), gx_rows(1, 48, 48), dev(dx=-1))

    def g3():
        arrived(("gx", "R"), 1, gx_rows(-2, 0, 48))
        arrived(("gx", "L"), 1, gx_rows(2, 48, 48))
        for b in range(3):
            part = slice(b * BLOCK, (b + 1) * BLOCK)
            grt[:, part] = gr[part, :].T

    def halves(u):
        return REDUCE[u][0], range(REDUCE[u][1], REDUCE[u][1] + REDUCE[u][2]), pl.ds(REDUCE[u][1], REDUCE[u][2])

    def s0(u):
        t, hs, ds = halves(u)
        for half, out in ((sib, po), (core, pm)):
            for h in hs:
                b = gs[t, :, :, :, h * 256:(h + 1) * 256].reshape(1024, 256)
                r = jnp.dot(at[half], b, preferred_element_type=F32)
                for xx in range(NX):
                    part = r[:, xx * 64:(xx + 1) * 64]
                    out[t, h, xx] = jnp.concatenate([part[:192], part[192:]], axis=1)
            if out is po:
                send(("cx", u), 0, po.at[t, ds], cx.at[t, ds], dev(other=True))

    xp, xm, xo = near("x", 1), near("x", -1), near("x", 2)
    A, B, ALL = pl.ds(0, 96), pl.ds(96, 96), pl.ds(0, 192)

    def s1(u):
        t, hs, ds = halves(u)
        arrived(("cx", u), 0, cx.at[t, ds])
        name = ("x", u)

        def add(xx):
            for h in hs:
                pm[t, h, xx] += cx[t, h, xx]

        add(xo)
        if REDUCE[u][3]:
            send(name, 0, pm.at[t, ds, xo], xr.at[t, ds, 0], dev(dx=2))
            add(xp)
            send(name, 1, pm.at[t, ds, xp], xr.at[t, ds, 1], dev(dx=1))
            add(xm)
            send(name, 2, pm.at[t, ds, xm], xr.at[t, ds, 2], dev(dx=-1))
        else:
            send(name, 0, pm.at[t, ds, xo, A], xr.at[t, ds, 0, A], dev(dx=1))
            send(name, 3, pm.at[t, ds, xo, B], xr.at[t, ds, 0, B], dev(dx=-1))
            add(xp)
            send(name, 1, pm.at[t, ds, xp, B], xr.at[t, ds, 1, B], dev(dx=1))
            add(xm)
            send(name, 4, pm.at[t, ds, xm, A], xr.at[t, ds, 2, A], dev(dx=-1))
        add(x)

    def s2(u):
        t, hs, ds = halves(u)
        name = ("x", u)
        arrived(name, 0, xr.at[t, ds, 0, A])
        for h in hs:
            pm[t, h, xp, A] += xr[t, h, 0, A]
        send(name, 2, pm.at[t, ds, xp, A], xr.at[t, ds, 1, A], dev(dx=1))
        arrived(name, 3, xr.at[t, ds, 0, B])
        for h in hs:
            pm[t, h, xm, B] += xr[t, h, 0, B]
        send(name, 5, pm.at[t, ds, xm, B], xr.at[t, ds, 2, B], dev(dx=-1))

    def s3(u):
        t, hs, ds = halves(u)
        name = ("x", u)
        if REDUCE[u][3]:
            for k in range(3):
                arrived(name, k, xr.at[t, ds, k])
        else:
            arrived(name, 1, xr.at[t, ds, 1, B])
            arrived(name, 4, xr.at[t, ds, 2, A])
            arrived(name, 2, xr.at[t, ds, 1, A])
            arrived(name, 5, xr.at[t, ds, 2, B])
        pieces = []
        for h in hs:
            total = pm[t, h, x] + (xr[t, h, 1] + xr[t, h, 2])
            if REDUCE[u][3]:
                total = total + xr[t, h, 0]
            total = jnp.concatenate([total[:, :64], total[:, 64:]], axis=0)
            high = total.astype(BF16)
            pieces += [high, (total - high.astype(F32)).astype(BF16)]
        r = jnp.dot(grt[...], jnp.concatenate(pieces, axis=1), preferred_element_type=F32)
        for n, h in enumerate(hs):
            v = (r[:, n * BLOCK:n * BLOCK + 64] + r[:, n * BLOCK + 64:(n + 1) * BLOCK]).reshape(32, 2, 24, 64)
            v = jnp.concatenate([v[:, 0], v[:, 1]], axis=2).reshape(NY, NC, 2, 24, BLOCK)
            for k in range(NC):
                q[t, h, k] = v[:, k]
        send(("qc", u), 0, q.at[t, ds, sib], qcr.at[t, ds], dev(other=True))

    def q_to(u, dy, p=None):
        t, hs, ds = halves(u)
        return q.at[t, ds, core, near("y", dy), pl.ds(0, 2) if p is None else pl.ds(p, 1)]

    def y_slot(u, k, p=None):
        t, hs, ds = halves(u)
        return yr.at[t, ds, k, pl.ds(0, 2) if p is None else pl.ds(p, 1)]

    def s4(u):
        t, hs, ds = halves(u)
        arrived(("qc", u), 0, qcr.at[t, ds])
        for h in hs:
            q[t, h, core] += qcr[t, h]
        if REDUCE[u][4]:
            for d in (4, 3, 5, 2, 6, 1, 7):
                send(("q", u), d, q_to(u, d), y_slot(u, d), dev(dy=d))
        else:
            send(("q", u), 0, q_to(u, 4, 0), y_slot(u, 0, 0), dev(dy=1))
            send(("q", u), 4, q_to(u, -4, 1), y_slot(u, 4, 1), dev(dy=-1))

    def y_step(u, k):
        if REDUCE[u][4]:
            return
        for side, sign in ((0, 1), (1, -1)):
            p = side if k == 1 else None
            slot = y_slot(u, 4 * side + k - 1, p)
            arrived(("q", u), 4 * side + k - 1, slot)
            own = q_to(u, sign * (4 - k), p)
            own[...] += slot[...]
            send(("q", u), 4 * side + k, q_to(u, sign * (4 - k)), y_slot(u, 4 * side + k), dev(dy=sign))

    def s5(u):
        y_step(u, 1)

    def s6(u):
        y_step(u, 2)

    def s7(u):
        y_step(u, 3)

    def s8(u):
        t, hs, ds = halves(u)
        slots = range(1, 8) if REDUCE[u][4] else (3, 7)
        for k in slots:
            arrived(("q", u), k, y_slot(u, k))
        for h in hs:
            total = q[t, h, core, y]
            for k in slots:
                total = total + yr[t, h, k]
            fin[t, h] = total
            for b in range(2):
                last = f_copy(t, h, b)
                if t < 2:
                    last.start()
                else:
                    mine = f_mine(h, b)
                    pl.when(jnp.logical_not(mine))(last.start)

                    @pl.when(mine)
                    def _():
                        zr[2, 0] = fin[2, h, b]

    def f_mine(h, b):
        return jnp.logical_and(zl == 2 * core + b, core == h)

    def f_copy(t, h, b):
        zz = 2 * core + b
        i = lax.rem(zz - zl + NZL, NZL)
        return copy_of("f", t * 4 + h * 2 + b, fin.at[t, h, b], zr.at[t, i],
                       at_device(x, y, zz, near("zh", t + 1), h), rk=t * 4 + i)

    def finish():
        for t in range(NT):
            for i in range(NZL):
                def wait(t=t, i=i):
                    arrived("f", t * 4 + i, zr.at[t, i])
                if t < 2 or i:
                    wait()
                else:
                    pl.when(core != zl // 2)(wait)
        total = zr[0, 0]
        for n in range(1, 12):
            total = total + zr[n // 4, n % 4]
        out_ref[0:24, :] = total[:, :64]
        out_ref[24:48, :] = total[:, 64:]
        for t in range(NT):
            for h in range(NC):
                for b in range(2):
                    last = f_copy(t, h, b)
                    if t < 2:
                        last.wait_send()
                    else:
                        pl.when(jnp.logical_not(f_mine(h, b)))(last.wait_send)

    z0(0)
    prepare_a()
    z0(1)
    z0(2)
    g0()
    z0(3)
    z0(4)
    z0(5)
    o1(0,0)
    o1(1,0)
    o1(0,1)
    o1(2,0)
    o1(1,1)
    fw(0,2,"R",0)
    fw(0,2,"L",0)
    o1(2,1)
    fw(1,2,"R",0)
    fw(1,2,"L",0)
    fw(0,2,"R",1)
    fw(0,2,"L",1)
    fw(2,2,"R",0)
    fw(2,2,"L",0)
    fw(1,2,"R",1)
    fw(1,2,"L",1)
    fw(0,3,"R",0)
    fw(0,3,"L",0)
    fw(2,2,"R",1)
    fw(2,2,"L",1)
    fw(1,3,"R",0)
    fw(1,3,"L",0)
    fw(0,3,"R",1)
    fw(0,3,"L",1)
    fw(2,3,"R",0)
    fw(2,3,"L",0)
    fw(1,3,"R",1)
    fw(1,3,"L",1)
    fw(0,4,"R",0)
    o1(3,0)
    fw(2,3,"R",1)
    fw(2,3,"L",1)
    o1(4,0)
    fw(1,4,"R",0)
    g1()
    o1(3,1)
    fw(0,4,"L",1)
    o1(5,0)
    fw(2,4,"R",0)
    o1(4,1)
    fw(1,4,"L",1)
    o1(5,1)
    fw(3,2,"L",0)
    fw(3,2,"R",0)
    fw(2,4,"L",1)
    fw(4,2,"L",0)
    fw(4,2,"R",0)
    fw(3,2,"L",1)
    h5(0)
    s0(0)
    fw(3,2,"R",1)
    fw(5,2,"L",0)
    fw(5,2,"R",0)
    fw(4,2,"L",1)
    h5(1)
    s0(1)
    s1(0)
    fw(3,3,"L",0)
    g2()
    fw(4,2,"R",1)
    h5(2)
    fw(3,3,"R",0)
    s0(2)
    s1(1)
    fw(3,3,"L",1)
    fw(3,3,"R",1)
    fw(4,3,"R",0)
    fw(4,3,"L",0)
    fw(5,2,"L",1)
    fw(5,3,"L",0)
    fw(5,3,"R",0)
    s2(0)
    s1(2)
    fw(3,4,"R",0)
    fw(4,3,"R",1)
    fw(4,3,"L",1)
    fw(5,2,"R",1)
    fw(3,4,"L",1)
    fw(4,4,"R",0)
    fw(5,3,"L",1)
    fw(5,4,"R",0)
    g3()
    fw(4,4,"L",1)
    s2(1)
    h5(3)
    s0(3)
    fw(5,3,"R",1)
    fw(5,4,"L",1)
    s3(0)
    s1(3)
    s2(2)
    h5(4)
    s4(0)
    s0(4)
    s3(1)
    h5(5)
    s0(5)
    s2(3)
    s5(0)
    s4(1)
    s1(4)
    s1(5)
    s3(2)
    s6(0)
    s5(1)
    s3(3)
    s4(2)
    s4(3)
    s7(0)
    s6(1)
    s3(4)
    s5(2)
    s5(3)
    s4(4)
    s8(0)
    s7(1)
    s3(5)
    s6(2)
    s6(3)
    s4(5)
    s8(4)
    s8(1)
    s7(2)
    s7(3)
    s8(5)
    s8(2)
    s8(3)
    finish()
    drain()


def body(curl_tiles, gradient, a_pattern, g_pattern):
    hbm = pl.BlockSpec(memory_space=pl.ANY)
    return pl.pallas_call(
        kernel,
        out_shape=jax.ShapeDtypeStruct((48, 64), F32),
        in_specs=[hbm] * 4,
        out_specs=pl.BlockSpec(memory_space=pltpu.VMEM),
        scratch_shapes=[
            pltpu.VMEM((32, 32, 768), BF16),
            pltpu.VMEM((32, 1536), BF16),
            pltpu.VMEM((192, 192), jnp.int32),
            pltpu.VMEM((12, 192), jnp.int32),
            pltpu.VMEM((2, 384, 1024), BF16),
            pltpu.VMEM((32, 1536), BF16),
            pltpu.VMEM((NT, NY, NZL, 32, 512), BF16),
            pltpu.VMEM((384, 1536), BF16),
            pltpu.VMEM((1536, 384), BF16),
            pltpu.VMEM((NT, 2, NX, 192, BLOCK), F32),
            pltpu.VMEM((NT, 2, NX, 192, BLOCK), F32),
            pltpu.VMEM((NT, 2, NX, 192, BLOCK), F32),
            pltpu.VMEM((NT, 2, 3, 192, BLOCK), F32),
            pltpu.VMEM((NT, 2, NC, NY, 2, 24, BLOCK), F32),
            pltpu.VMEM((NT, 2, NY, 2, 24, BLOCK), F32),
            pltpu.VMEM((NT, 2, 8, 2, 24, BLOCK), F32),
            pltpu.VMEM((NT, NZL, 24, BLOCK), F32),
            pltpu.VMEM((NT, 2, 2, 24, BLOCK), F32),
            pltpu.SemaphoreType.DMA((4,)),
            pltpu.SemaphoreType.DMA((TOTAL,)),
            pltpu.SemaphoreType.DMA((TOTAL,)),
        ],
        compiler_params=pltpu.CompilerParams(
            collective_id=0, has_side_effects=True, vmem_limit_bytes=60 * 1024 * 1024),
    )(curl_tiles, gradient, a_pattern, g_pattern.T)


def solution(mesh):
    placed = (P(None, "col", "row"), P(("row", "col"), None), P(), P())
    return jax.shard_map(
        body, mesh=mesh, in_specs=placed, out_specs=P("row", "col"), check_vma=False
    )
```

time: 598 us -> 102 us (0.17)
  the two profiles are of different devices: /device:TPU:4 before, /device:TPU:1 now
where the time goes in v2:
time: 102 us
  Pallas kernels  100 us (98%)
  local copies, waits for them, and re-layouts  1.35 us (1%)
    pallas_call x1, Pallas kernels, body(): pl.pallas_call(kernel, out_shape=jax.ShapeDtypeStruct((48, 64), F32), in_...  100 us

profile of v2, /device:TPU:1, one launch (start us, length us, event | category | flops | bytes accessed | tf_op | source)
XLA Modules:
  0.0 101.8 jit_solution(5196563289212564261)
XLA Ops:
  0.0 100.4 %shard_map.46 = f32[48,64]{1,0:T(8,128)} custom-call(bf16[32,32,768]{2,1,0:T(8,128)(2,1)} %a_hbm.1, bf16[32,1536]{1,0:T(8,128)(2,1)} %g_hbm.1, s32[192,192]{1,0:T(8,128)} %ap_hbm.1, s32[12,192]{1,0:T(8,128)} %bitcast.1), custom_call_target="tpu_custom_call" | custom-call | tf_op jit(solution)/shard_map/pallas_call | solution.py:521
  100.4 1.3 %copy.6 = f32[48,64]{1,0:T(8,128)} copy(f32[48,64]{1,0:T(8,128)} %shard_map.46) | data formatting | bytes 24576

commit v3 on v2

--- a/solution.py
+++ b/solution.py
@@ -386,130 +386,130 @@
     z0(4)
     z0(5)
     o1(0,0)
+    o1(0,1)
     o1(1,0)
-    o1(0,1)
-    o1(2,0)
     o1(1,1)
     fw(0,2,"R",0)
     fw(0,2,"L",0)
-    o1(2,1)
+    fw(0,2,"R",1)
+    fw(0,2,"L",1)
     fw(1,2,"R",0)
     fw(1,2,"L",0)
-    fw(0,2,"R",1)
-    fw(0,2,"L",1)
+    fw(1,2,"R",1)
+    fw(1,2,"L",1)
+    o1(2,0)
+    o1(2,1)
+    fw(0,3,"R",0)
+    fw(0,3,"L",0)
+    fw(0,3,"R",1)
+    fw(0,3,"L",1)
+    fw(1,3,"R",0)
+    fw(1,3,"L",0)
+    fw(1,3,"R",1)
+    fw(1,3,"L",1)
     fw(2,2,"R",0)
     fw(2,2,"L",0)
-    fw(1,2,"R",1)
-    fw(1,2,"L",1)
-    fw(0,3,"R",0)
-    fw(0,3,"L",0)
     fw(2,2,"R",1)
     fw(2,2,"L",1)
-    fw(1,3,"R",0)
-    fw(1,3,"L",0)
-    fw(0,3,"R",1)
-    fw(0,3,"L",1)
+    o1(3,0)
+    fw(0,4,"R",0)
+    fw(0,4,"L",1)
+    g1()
+    fw(1,4,"R",0)
+    o1(3,1)
+    o1(5,0)
+    fw(1,4,"L",1)
     fw(2,3,"R",0)
     fw(2,3,"L",0)
-    fw(1,3,"R",1)
-    fw(1,3,"L",1)
-    fw(0,4,"R",0)
-    o1(3,0)
     fw(2,3,"R",1)
     fw(2,3,"L",1)
-    o1(4,0)
-    fw(1,4,"R",0)
-    g1()
-    o1(3,1)
-    fw(0,4,"L",1)
-    o1(5,0)
-    fw(2,4,"R",0)
-    o1(4,1)
-    fw(1,4,"L",1)
     o1(5,1)
+    fw(3,2,"R",0)
     fw(3,2,"L",0)
-    fw(3,2,"R",0)
-    fw(2,4,"L",1)
-    fw(4,2,"L",0)
-    fw(4,2,"R",0)
-    fw(3,2,"L",1)
     h5(0)
     s0(0)
+    fw(3,2,"L",1)
     fw(3,2,"R",1)
     fw(5,2,"L",0)
     fw(5,2,"R",0)
-    fw(4,2,"L",1)
     h5(1)
     s0(1)
+    fw(2,4,"R",0)
     s1(0)
+    fw(2,4,"L",1)
+    fw(5,2,"R",1)
+    fw(5,2,"L",1)
+    s1(1)
     fw(3,3,"L",0)
     g2()
+    fw(3,3,"R",0)
+    fw(3,3,"R",1)
+    fw(3,3,"L",1)
+    o1(4,0)
+    o1(4,1)
+    fw(5,3,"R",0)
+    fw(5,3,"L",0)
+    s2(0)
+    h5(2)
+    s0(2)
+    fw(5,3,"R",1)
+    fw(5,3,"L",1)
+    fw(3,4,"R",0)
+    s2(1)
+    fw(3,4,"L",1)
+    s1(2)
+    fw(4,2,"L",0)
+    fw(4,2,"R",0)
     fw(4,2,"R",1)
-    h5(2)
-    fw(3,3,"R",0)
-    s0(2)
-    s1(1)
-    fw(3,3,"L",1)
-    fw(3,3,"R",1)
-    fw(4,3,"R",0)
-    fw(4,3,"L",0)
-    fw(5,2,"L",1)
-    fw(5,3,"L",0)
-    fw(5,3,"R",0)
-    s2(0)
-    s1(2)
-    fw(3,4,"R",0)
-    fw(4,3,"R",1)
-    fw(4,3,"L",1)
-    fw(5,2,"R",1)
-    fw(3,4,"L",1)
-    fw(4,4,"R",0)
-    fw(5,3,"L",1)
+    fw(4,2,"L",1)
     fw(5,4,"R",0)
-    g3()
-    fw(4,4,"L",1)
-    s2(1)
+    fw(5,4,"L",1)
     h5(3)
     s0(3)
-    fw(5,3,"R",1)
-    fw(5,4,"L",1)
+    g3()
+    fw(4,3,"L",0)
+    fw(4,3,"R",0)
+    fw(4,3,"R",1)
     s3(0)
+    fw(4,3,"L",1)
     s1(3)
+    s3(1)
+    s4(0)
     s2(2)
-    h5(4)
-    s4(0)
-    s0(4)
-    s3(1)
     h5(5)
     s0(5)
+    fw(4,4,"R",0)
+    s4(1)
+    fw(4,4,"L",1)
     s2(3)
+    s1(5)
     s5(0)
-    s4(1)
+    s5(1)
+    s3(2)
+    h5(4)
+    s0(4)
+    s3(3)
+    s6(0)
+    s4(2)
+    s6(1)
     s1(4)
-    s1(5)
-    s3(2)
-    s6(0)
-    s5(1)
-    s3(3)
-    s4(2)
     s4(3)
     s7(0)
-    s6(1)
+    s5(2)
+    s3(5)
+    s7(1)
+    s5(3)
+    s4(5)
+    s8(0)
+    s6(2)
+    s8(1)
     s3(4)
-    s5(2)
-    s5(3)
+    s6(3)
     s4(4)
-    s8(0)
-    s7(1)
-    s3(5)
-    s6(2)
-    s6(3)
-    s4(5)
-    s8(4)
-    s8(1)
+    s8(5)
     s7(2)
     s7(3)
-    s8(5)
+    s8(4)
     s8(2)
     s8(3)
     finish()

time: 102 us -> 101 us (level)
    pallas_call x1, Pallas kernels: 100 us -> 99.3 us  [body(): pl.pallas_call(kernel, out_shape=jax.ShapeDtypeStruct((48, 64), F32), in_...]
where the time goes in v3:
time: 101 us
  Pallas kernels  99.3 us (98%)
  local copies, waits for them, and re-layouts  1.35 us (1%)
    pallas_call x1, Pallas kernels, body(): pl.pallas_call(kernel, out_shape=jax.ShapeDtypeStruct((48, 64), F32), in_...  99.3 us

profile of v3, /device:TPU:1, one launch (start us, length us, event | category | flops | bytes accessed | tf_op | source)
XLA Modules:
  0.0 100.7 jit_solution(740690375577158066)
XLA Ops:
  0.0 99.3 %shard_map.46 = f32[48,64]{1,0:T(8,128)} custom-call(bf16[32,32,768]{2,1,0:T(8,128)(2,1)} %a_hbm.1, bf16[32,1536]{1,0:T(8,128)(2,1)} %g_hbm.1, s32[192,192]{1,0:T(8,128)} %ap_hbm.1, s32[12,192]{1,0:T(8,128)} %bitcast.1), custom_call_target="tpu_custom_call" | custom-call | tf_op jit(solution)/shard_map/pallas_call | solution.py:521
  99.3 1.3 %copy.6 = f32[48,64]{1,0:T(8,128)} copy(f32[48,64]{1,0:T(8,128)} %shard_map.46) | data formatting | bytes 24576

commit v4 on v3

--- a/solution.py
+++ b/solution.py
@@ -107,11 +107,13 @@
         part = slice(p * BLOCK, (p + 1) * BLOCK)
         gm[:, part] = (g_buf[:, part].astype(F32) * jnp.broadcast_to(keep[p:p + 1, :], (32, BLOCK))).astype(BF16)
     me_m = x * NZH + zh
-    gr[pl.ds(pl.multiple_of(me_m * 32, 32), 32), :] = gm[...]
-    for t in range(NT):
+
+    def lay_out(t):
         jj = near("zh", 1 + t)
         blocks = [gm[:, pl.ds(pl.multiple_of(xx * 384 + jj * BLOCK, BLOCK), BLOCK)] for xx in range(NX)]
         gs[t, y, zl] = jnp.concatenate([b[:, h * 64:(h + 1) * 64] for h in range(2) for b in blocks], axis=1)
+
+    lay_out(0)
 
     pl.semaphore_wait(barrier, len(peers))
 
@@ -378,13 +380,16 @@
                         pl.when(jnp.logical_not(f_mine(h, b)))(last.wait_send)
 
     z0(0)
-    prepare_a()
+    lay_out(1)
+    lay_out(2)
+    gr[pl.ds(pl.multiple_of(me_m * 32, 32), 32), :] = gm[...]
     z0(1)
     z0(2)
     g0()
     z0(3)
     z0(4)
     z0(5)
+    prepare_a()
     o1(0,0)
     o1(0,1)
     o1(1,0)

time: 101 us -> 101 us (level)
  no operation moved by 1% of the time
where the time goes in v4:
time: 101 us
  Pallas kernels  99.3 us (98%)
  local copies, waits for them, and re-layouts  1.35 us (1%)
    pallas_call x1, Pallas kernels, body(): pl.pallas_call(kernel, out_shape=jax.ShapeDtypeStruct((48, 64), F32), in_...  99.3 us

profile of v4, /device:TPU:1, one launch (start us, length us, event | category | flops | bytes accessed | tf_op | source)
XLA Modules:
  0.0 100.7 jit_solution(6114337252171397542)
XLA Ops:
  0.0 99.3 %shard_map.46 = f32[48,64]{1,0:T(8,128)} custom-call(bf16[32,32,768]{2,1,0:T(8,128)(2,1)} %a_hbm.1, bf16[32,1536]{1,0:T(8,128)(2,1)} %g_hbm.1, s32[192,192]{1,0:T(8,128)} %ap_hbm.1, s32[12,192]{1,0:T(8,128)} %bitcast.1), custom_call_target="tpu_custom_call" | custom-call | tf_op jit(solution)/shard_map/pallas_call | solution.py:526
  99.3 1.3 %copy.6 = f32[48,64]{1,0:T(8,128)} copy(f32[48,64]{1,0:T(8,128)} %shard_map.46) | data formatting | bytes 24576
